TPU v7x, 32 devices: a whole 2x2x4 slice. The times are simulated.
32 devices in a mesh: dp: 8 (over y, x, core), mp: 4 (over z).
Axes of the slice: x: 2, y: 2, z: 4, core: 2. Of those that a mesh axis runs over, the one named last changes fastest.
Arguments:
- tokens: bfloat16 [32768, 768], P(('dp', 'mp')), may hold values from -6 to 6
- block_kind: int32 [64], P(('dp', 'mp')), may hold values from 0 to 2
- ln1_gain: bfloat16 [768], replicated, may hold values from 0.099609375 to 1.8984375
- ln1_bias: bfloat16 [768], replicated, may hold values from -3 to 3
- w_in: bfloat16 [768, 3072], P(None, 'mp'), may hold values from -0.21875 to 0.21875
- b_in: bfloat16 [3072], P('mp'), may hold values from -3 to 3
- w_out: bfloat16 [3072, 768], P('mp'), may hold values from -0.21875 to 0.21875
- b_out: bfloat16 [768], replicated, may hold values from -3 to 3
- ln2_gain: bfloat16 [768], replicated, may hold values from 0.099609375 to 1.8984375
- ln2_bias: bfloat16 [768], replicated, may hold values from -3 to 3
- grad_out: bfloat16 [32768, 768], P(('dp', 'mp')), may hold values from -6 to 6
Outputs:
- output: bfloat16 [32768, 768], P(('dp', 'mp'))
- grad_tokens: float32 [32768, 768], P(('dp', 'mp'))
- grad_ln1_gain: float32 [768], replicated
- grad_ln1_bias: float32 [768], replicated
- grad_w_in: float32 [768, 3072], P(None, 'mp')
- grad_b_in: float32 [3072], P('mp')
- grad_w_out: float32 [3072, 768], P('mp')
- grad_b_out: float32 [768], replicated
- grad_ln2_gain: float32 [768], replicated
- grad_ln2_bias: float32 [768], replicated
Inputs may be any that keep to these rules, and one draw needn't show every extreme that they name: The sequences of block b have 512 // 2 ** block_kind[b] tokens each and fill the block.
All inputs are finite; a program needn't handle non-finite values.
Results may differ from a plain program's by a relative error of at most 0.0095.
Values may be sent and summed in bfloat16 or wider, within the bound.
A program may use at most 128 MiB of HBM per device.

v0:
```python
import math

import jax
import jax.numpy as jnp
from jax import lax
from jax.sharding import PartitionSpec as P

D = 768
BLOCK = 512


def sequence_tables(block_len):
    row_ids = jnp.arange(block_len, dtype=jnp.int32)
    cosines = []
    sines = []
    for variant in range(3):
        seq_len = block_len // 2**variant
        places = row_ids % seq_len
        owners = row_ids // seq_len
        same_seq = owners[:, None] == owners[None, :]
        phase = places[:, None] * places[None, :] % seq_len
        angle = phase.astype(jnp.float32) * (2.0 * math.pi / seq_len)
        factor = 1.0 / math.sqrt(seq_len)
        cosines.append(jnp.where(same_seq, jnp.cos(angle) * factor, 0.0))
        sines.append(jnp.where(same_seq, jnp.sin(angle) * factor, 0.0))
    return (jnp.stack(cosines), jnp.stack(sines))


def width_tables(count):
    row_ids = jnp.arange(count, dtype=jnp.int32)
    phase = row_ids[:, None] * row_ids[None, :] % count
    angle = phase.astype(jnp.float32) * (2.0 * math.pi / count)
    factor = 1.0 / math.sqrt(count)
    return (jnp.cos(angle) * factor, jnp.sin(angle) * factor)


def layer_norm(values, gain, shift):
    centre = values - jnp.mean(values, axis=-1, keepdims=True)
    spread = jnp.mean(centre * centre, axis=-1, keepdims=True)
    return centre * lax.rsqrt(spread + 1e-05) * gain + shift


def gelu_tanh(values):
    return jax.nn.gelu(values, approximate=True)


def contract_rows(left, right):
    return lax.dot_general(
        left, right, (((0,), (0,)), ((), ())), preferred_element_type=jnp.float32
    )


def times_transposed(left, right):
    return lax.dot_general(
        left, right, (((1,), (1,)), ((), ())), preferred_element_type=jnp.float32
    )


def local(
    tokens, block_kind, ln1_gain, ln1_bias, w_in, b_in, w_out, b_out, ln2_gain, ln2_bias, grad_out
):
    low_type = jnp.bfloat16
    full_type = jnp.float32
    cos_all, sin_all = sequence_tables(BLOCK)
    cos_feat, sin_feat = width_tables(D)
    cos_feat = cos_feat.astype(low_type)
    sin_feat = sin_feat.astype(low_type)
    seq_cos = cos_all.astype(low_type)[block_kind]
    seq_sin = sin_all.astype(low_type)[block_kind]
    row_count = tokens.shape[0]
    block_count = row_count // BLOCK
    by_cos = (
        jnp.dot(tokens, cos_feat, preferred_element_type=full_type)
        .astype(low_type)
        .reshape(block_count, BLOCK, D)
    )
    by_sin = (
        jnp.dot(tokens, sin_feat, preferred_element_type=full_type)
        .astype(low_type)
        .reshape(block_count, BLOCK, D)
    )
    mixed = jnp.einsum(
        "bst,btd->bsd", seq_cos, by_cos, preferred_element_type=full_type
    ) - jnp.einsum("bst,btd->bsd", seq_sin, by_sin, preferred_element_type=full_type)
    summed = tokens.astype(full_type) + mixed.reshape(row_count, D)
    normed, norm_one_back = jax.vjp(
        layer_norm, summed, ln1_gain.astype(full_type), ln1_bias.astype(full_type)
    )
    normed_low = normed.astype(low_type)
    ff_rows = lax.all_gather(normed_low, "mp", axis=0, tiled=True)
    in_weight, in_bias, out_weight = (w_in, b_in, w_out)
    hidden_pre = jnp.dot(ff_rows, in_weight, preferred_element_type=full_type) + in_bias.astype(
        full_type
    )
    hidden_act, gelu_back = jax.vjp(gelu_tanh, hidden_pre)
    hidden_low = hidden_act.astype(low_type)
    branch_part = jnp.dot(hidden_low, out_weight, preferred_element_type=full_type)
    branch = lax.psum_scatter(branch_part, "mp", scatter_dimension=0, tiled=True) + b_out.astype(
        full_type
    )
    result, norm_two_back = jax.vjp(
        layer_norm, normed + branch, ln2_gain.astype(full_type), ln2_bias.astype(full_type)
    )
    grad_residual, grad_gain_two, grad_shift_two = norm_two_back(grad_out.astype(full_type))
    grad_branch = grad_residual.astype(low_type)
    grad_bias_out = jnp.sum(grad_branch, axis=0, dtype=full_type)
    grad_rows = lax.all_gather(grad_branch, "mp", axis=0, tiled=True)
    grad_weight_out = contract_rows(hidden_low, grad_rows)
    grad_hidden = times_transposed(grad_rows, out_weight)
    grad_pre = gelu_back(grad_hidden)[0].astype(low_type)
    grad_weight_in = contract_rows(ff_rows, grad_pre)
    grad_bias_in = jnp.sum(grad_pre, axis=0, dtype=full_type)
    normed_part = times_transposed(grad_pre, in_weight)
    grad_from_ff = lax.psum_scatter(
        normed_part.astype(jnp.bfloat16), "mp", scatter_dimension=0, tiled=True
    ).astype(jnp.float32)
    grad_summed, grad_gain_one, grad_shift_one = norm_one_back(grad_residual + grad_from_ff)
    grad_mixed = grad_summed.astype(low_type).reshape(block_count, BLOCK, D)
    grad_cos = jnp.einsum(
        "bts,btd->bsd", seq_cos, grad_mixed, preferred_element_type=full_type
    ).astype(low_type)
    grad_sin = (
        -jnp.einsum("bts,btd->bsd", seq_sin, grad_mixed, preferred_element_type=full_type)
    ).astype(low_type)
    grad_tokens = (
        grad_summed
        + times_transposed(grad_cos.reshape(row_count, D), cos_feat)
        + times_transposed(grad_sin.reshape(row_count, D), sin_feat)
    )
    grad_weight_in, grad_weight_out, grad_bias_in = lax.psum(
        (grad_weight_in, grad_weight_out, grad_bias_in), "dp"
    )
    grad_gain_one, grad_shift_one, grad_gain_two, grad_shift_two, grad_bias_out = lax.psum(
        (grad_gain_one, grad_shift_one, grad_gain_two, grad_shift_two, grad_bias_out), ("dp", "mp")
    )
    return (
        result.astype(low_type),
        grad_tokens,
        grad_gain_one,
        grad_shift_one,
        grad_weight_in,
        grad_bias_in,
        grad_weight_out,
        grad_bias_out,
        grad_gain_two,
        grad_shift_two,
    )


def solution(mesh):
    in_specs = (
        P(("dp", "mp"), None),
        P(("dp", "mp")),
        P(),
        P(),
        P(None, "mp"),
        P("mp"),
        P("mp", None),
        P(),
        P(),
        P(),
        P(("dp", "mp"), None),
    )
    out_specs = (
        P(("dp", "mp"), None),
        P(("dp", "mp"), None),
        P(),
        P(),
        P(None, "mp"),
        P("mp"),
        P("mp", None),
        P(),
        P(),
        P(),
    )
    return jax.shard_map(local, mesh=mesh, in_specs=in_specs, out_specs=out_specs, check_vma=False)
```

profile of v0, /device:TPU:0, one launch (start us, length us, event | category | flops | bytes accessed | tf_op | source)
XLA Modules:
  0.0 787.7 jit_solution(9888564121610109268)
XLA Ops:
  7.3 12.8 %fusion.17 = bf16[1024,768]{0,1:T(8,128)(2,1)} fusion(bf16[1024,768]{1,0:T(8,128)(2,1)} %param.11), kind=kOutput, calls=%fused_computation.68 | convolution fusion | flops 1215234048 | bytes 3145728 | tf_op jit(solution)/shard_map/dot_general | solution.py:73
  20.1 12.6 %fusion.18 = bf16[1024,768]{0,1:T(8,128)(2,1)} fusion(bf16[1024,768]{1,0:T(8,128)(2,1)S(1)} %copy-done.13), kind=kOutput, calls=%fused_computation.69 | convolution fusion | flops 1215234048 | bytes 3145728 | tf_op jit(solution)/shard_map/dot_general | solution.py:78
  34.4 4.8 fusion.21
  39.3 4.8 fusion.23
  44.1 4.8 fusion.25
  56.9 3.1 copy.32
  67.6 118.1 %all-gather.3.cloned.1.call-done = bf16[4096,768]{1,0:T(8,128)(2,1)} async-done(((bf16[1024,768]{1,0:T(8,128)(2,1)}), bf16[4096,768]{1,0:T(8,128)(2,1)}) %all-gather.3.cloned.1.call-update) | async-done | bytes 6291472 | tf_op jit(solution)/shard_map/all_gather | solution.py:90
  185.7 12.0 %multiply_convert_fusion = (bf16[4096,768]{1,0:T(8,128)(2,1)S(1)}, f32[4096,768]{1,0:T(8,128)}) fusion(f32[768]{0:T(1024)S(1)} %convert_element_type.155, bf16[4096,768]{1,0:T(8,128)(2,1)} %all-gather.3.cloned.1.call-done, bf16[768,768]{1,0:T(8,128)(2,1)S(1)} %copy-done), kind=kOutput, calls=%fused_computation.12 | convolution fusion | flops 4863295488 | bytes 26348544 | tf_op jit(solution)/shard_map/dot_general | solution.py:92
  200.4 8.0 %fusion.72 = f32[4096,768]{1,0:T(8,128)} fusion(bf16[4096,768]{1,0:T(8,128)(2,1)S(1)} %get-tuple-element.42, bf16[768,768]{1,0:T(8,128)(2,1)S(1)} %copy-done.21), kind=kOutput, calls=%fused_computation.150 | convolution fusion | flops 4831838208 | bytes 20054016 | tf_op jit(solution)/shard_map/dot_general | solution.py:97
  209.1 209.5 %reduce-scatter.3.cloned.1.call-done = f32[1024,768]{1,0:T(8,128)} async-done(((f32[4096,768]{1,0:T(8,128)}), f32[1024,768]{1,0:T(8,128)}) %reduce-scatter.3.cloned.1.call-update) | async-done | bytes 3145744 | tf_op jit(solution)/shard_map/reduce_scatter | solution.py:98
  418.7 3.9 fusion.69
  431.1 116.5 %all-gather.5.cloned.1.call-done = bf16[4096,768]{1,0:T(8,128)(2,1)} async-done(((bf16[1024,768]{1,0:T(8,128)(2,1)}), bf16[4096,768]{1,0:T(8,128)(2,1)}) %all-gather.5.cloned.1.call-update) | async-done | bytes 6291472 | tf_op jit(solution)/shard_map/all_gather | solution.py:107
  547.6 16.5 %convert_reduce_fusion = (f32[768]{0:T(1024)S(1)}, bf16[4096,768]{1,0:T(8,128)(2,1)S(1)}) fusion(f32[4096,768]{1,0:T(8,128)} %get-tuple-element.43, f32[768]{0:T(1024)S(1)} %convert_element_type.155, bf16[4096,768]{1,0:T(8,128)(2,1)} %all-gather.5.cloned.1.call-done, bf16[768,768]{1,0:T(8,128)(2,1)S(1)} %copy-done.21), kind=kOutput, calls=%fused_computation.11 | convolution fusion | flops 4904188928 | bytes 26351616 | tf_op jit(solution)/shard_map/dot_general | solution.py:54
  566.8 7.1 convolution_convert_fusion
  574.0 15.0 %psum.59 = f32[768]{0:T(1024)} all-reduce(f32[768]{0:T(1024)S(1)} %get-tuple-element.23), channel_id=1, replica_groups=mesh['dp'=8,'mp'=4] {'dp'}, use_global_device_ids=true, to_apply=%region_16.17 | all-reduce | flops 768 | bytes 6144 | tf_op jit(solution)/shard_map/psum | solution.py:130
  589.0 10.3 %fusion.74 = f32[768,768]{1,0:T(8,128)} fusion(bf16[4096,768]{1,0:T(8,128)(2,1)} %copy-done.23, bf16[4096,768]{1,0:T(8,128)(2,1)} %all-gather.5.cloned.1.call-done), kind=kOutput, calls=%fused_computation.152 | convolution fusion | flops 4831838208 | bytes 14942208 | tf_op jit(solution)/shard_map/dot_general | solution.py:48
  599.3 8.2 %fusion.73 = f32[768,768]{1,0:T(8,128)} fusion(bf16[4096,768]{1,0:T(8,128)(2,1)} %all-gather.3.cloned.1.call-done, bf16[4096,768]{1,0:T(8,128)(2,1)S(1)} %copy-done.25), kind=kOutput, calls=%fused_computation.151 | convolution fusion | flops 4831838208 | bytes 14942208 | tf_op jit(solution)/shard_map/dot_general | solution.py:48
  607.5 75.5 %reduce-scatter.5.cloned.1.call-done = bf16[1024,768]{1,0:T(8,128)(2,1)} async-done(((bf16[4096,768]{1,0:T(8,128)(2,1)}), bf16[1024,768]{1,0:T(8,128)(2,1)}) %reduce-scatter.5.cloned.1.call-update) | async-done | bytes 1572880 | tf_op jit(solution)/shard_map/reduce_scatter | solution.py:114
  683.0 4.3 multiply_reduce_fusion
  691.5 42.5 %all-reduce = (f32[768]{0:T(1024)}, f32[768]{0:T(1024)}, f32[768]{0:T(1024)}, f32[768]{0:T(1024)}, f32[768]{0:T(1024)}) all-reduce(f32[768]{0:T(1024)S(1)} %get-tuple-element.10, f32[768]{0:T(1024)S(1)} %get-tuple-element.14, f32[768]{0:T(1024)S(1)} %get-tuple-element.25, ...), channel_id=1, replica_groups=mesh['dp'=8,'mp'=4] {'dp','mp'}, use_global_device_ids=true, to_apply=%region_11.12 | all-reduce | flops 3840 | bytes 30720 | tf_op jit(solution)/shard_map/psum | solution.py:133
  738.5 12.6 %fusion.19 = f32[1024,768]{1,0:T(8,128)S(1)} fusion(bf16[1024,768]{1,0:T(8,128)(2,1)S(1)} %bitcast.41), kind=kOutput, calls=%fused_computation.76 | convolution fusion | flops 1214447616 | bytes 4718592 | tf_op jit(solution)/shard_map/dot_general | solution.py:54
  751.0 11.7 %add_add_fusion.2 = f32[1024,768]{1,0:T(8,128)} fusion(f32[1024,768]{1,0:T(8,128)S(1)} %fusion.19, f32[1024,768]{1,0:T(8,128)S(1)} %copy-done.5, bf16[1024,768]{1,0:T(8,128)(2,1)S(1)} %bitcast.40, f32[1024]{0:T(1024)S(1)} %negate_multiply_fusion), kind=kOutput, calls=%fused_computation.28 | convolution fusion | flops 1216806912 | bytes 11014144 | tf_op jit(solution)/shard_map/dot_general | solution.py:54
  762.7 13.2 %all-reduce.4.cloned.1.call-done = (f32[768,768]{1,0:T(8,128)}, f32[768,768]{1,0:T(8,128)}) async-done(((f32[768,768]{1,0:T(8,128)}, f32[768,768]{1,0:T(8,128)}), (f32[768,768]{1,0:T(8,128)}, f32[768,768]{1,0:T(8,128)})) %all-reduce.4.cloned.1.call-update) | async-done | bytes 4718608 | tf_op jit(solution)/shard_map/psum | solution.py:130
  775.9 3.4 copy.35
  (102 shorter events, 41.9 us)
Async XLA Ops:
  7.2 178.6 %copy-start = (bf16[768,768]{1,0:T(8,128)(2,1)S(1)}, bf16[768,768]{1,0:T(8,128)(2,1)}, u32[]{:S(2)}) copy-start(bf16[768,768]{1,0:T(8,128)(2,1)} %param.15) | copy-start | bytes 3538948
  7.2 178.5 %all-gather.3.cloned.1.call-start = ((), (), s32[]{:S(2)}) async-start(), calls=%async_computation.2 | async-start | bytes 7864320 | tf_op jit(solution)/shard_map/all_gather | solution.py:90
  7.3 12.8 %copy-start.13 = (bf16[1024,768]{1,0:T(8,128)(2,1)S(1)}, bf16[1024,768]{1,0:T(8,128)(2,1)}, u32[]{:S(2)}) copy-start(bf16[1024,768]{1,0:T(8,128)(2,1)} %param.11) | copy-start | bytes 4718596
  20.1 12.6 %copy-start.22 = (s32[2]{0:T(128)S(1)}, s32[2]{0:T(128)}, u32[]{:S(2)}) copy-start(s32[2]{0:T(128)} %param.12) | copy-start | bytes 28
  59.9 2.4 copy-start.7
  60.0 2.4 copy-start.9
  64.1 1.7 copy-start.1
  65.8 1.8 copy-start.17
  67.5 351.2 %reduce-scatter.3.cloned.1.call-start = ((), (), s32[]{:S(2)}) async-start(), calls=%async_computation.3 | async-start | bytes 15728640 | tf_op jit(solution)/shard_map/reduce_scatter | solution.py:98
  67.6 132.8 %copy-start.21 = (bf16[768,768]{1,0:T(8,128)(2,1)S(1)}, bf16[768,768]{1,0:T(8,128)(2,1)}, u32[]{:S(2)}) copy-start(bf16[768,768]{1,0:T(8,128)(2,1)} %param.17) | copy-start | bytes 3538948
  197.7 2.7 copy-start.23
  208.4 339.1 %all-gather.5.cloned.1.call-start = ((), (), s32[]{:S(2)}) async-start(), calls=%async_computation.4 | async-start | bytes 7864320 | tf_op jit(solution)/shard_map/all_gather | solution.py:107
  422.5 1.4 copy-start.8
  427.8 1.7 copy-start.3
  431.0 252.0 %reduce-scatter.5.cloned.1.call-start = ((), (), s32[]{:S(2)}) async-start(), calls=%async_computation.5 | async-start | bytes 7864320 | tf_op jit(solution)/shard_map/reduce_scatter | solution.py:114
  564.1 2.7 copy-start.24
  573.9 202.0 %all-reduce.4.cloned.1.call-start = ((), (), s32[]{:S(2)}) async-start(), calls=%async_computation.6 | async-start | bytes 9437184 | tf_op jit(solution)/shard_map/psum | solution.py:130
  589.0 10.3 %copy-start.25 = (bf16[4096,768]{1,0:T(8,128)(2,1)S(1)}, bf16[4096,768]{1,0:T(8,128)(2,1)}, u32[]{:S(2)}) copy-start(bf16[4096,768]{1,0:T(8,128)(2,1)} %copy-done.24) | copy-start | bytes 18874372
  683.0 4.3 copy-start.2
  683.0 5.2 copy-start.4
  683.0 5.6 copy-start.6
  691.5 44.7 %copy-start.10 = (bf16[2,512,512]{2,1,0:T(8,128)(2,1)S(1)}, bf16[2,512,512]{2,1,0:T(8,128)(2,1)}, u32[]{:S(2)}) copy-start(bf16[2,512,512]{2,1,0:T(8,128)(2,1)} %gather_fusion.1) | copy-start | bytes 3145732
  738.4 12.6 %copy-start.5 = (f32[1024,768]{1,0:T(8,128)S(1)}, f32[1024,768]{1,0:T(8,128)}, u32[]{:S(2)}) copy-start(f32[1024,768]{1,0:T(8,128)} %get-tuple-element.28) | copy-start | bytes 9437188
  775.9 3.4 copy-start.12
  (7 other events, 6.2 us)
Sparse Core Ops, SparseCore 0:
  67.6 118.0 all-gather.2
  208.6 210.0 reduce-scatter.2
  431.1 116.3 all-gather.4
  574.0 108.9 reduce-scatter.4
  686.8 89.0 all-reduce.3
where the time goes:
time: 795 us; the launch traced here: 788 us
  waiting for transfers between devices  533 us (67%)
  matrix products  117 us (15%)
  blocking collectives  57.5 us (7%)
  other arithmetic  38 us (5%)
  local copies, waits for them, and re-layouts  27.1 us (3%)
  between operations  14.7 us (2%)
    reduce_scatter x1, waiting for transfers between devices, local(): lax.psum_scatter(branch_part, 'mp', scatter_dimension=0, tiled=True)  210 us
    all_gather x1, waiting for transfers between devices, local(): ff_rows = lax.all_gather(normed_low, 'mp', axis=0, tiled=True)  118 us
    all_gather x1, waiting for transfers between devices, local(): grad_rows = lax.all_gather(grad_branch, 'mp', axis=0, tiled=True)  117 us
    reduce_scatter x1, waiting for transfers between devices, local(): lax.psum_scatter(normed_part.astype(jnp.bfloat16), 'mp', scatter_dimensio...  75.5 us
    dot_general x4, matrix products, times_transposed(): lax.dot_general(left, right, (((1,), (1,)), ((), ())), preferred_element_...  47.9 us
    psum x1, blocking collectives, local(): lax.psum((grad_gain_one, grad_shift_one, grad_gain_two, grad_shift_two, g...  42.5 us
    dot_general x2, matrix products, contract_rows(): lax.dot_general(left, right, (((0,), (0,)), ((), ())), preferred_element_...  18.5 us
    unnamed x54, local copies, waits for them, and re-layouts  16.4 us
  transfers between devices with their start and end apart: 5, of which 5 were waited for; matrix products, arithmetic and copies ran while one was open for 7% of the time, Pallas kernels for 0%

commit v1 on v0

v1 whole, which is shorter than its diff:
```python
import functools
import math

import jax
import jax.numpy as jnp
import numpy as np
from jax import lax
from jax.experimental import pallas as pl
from jax.experimental.pallas import tpu as pltpu
from jax.sharding import PartitionSpec as P

BLOCK = 512
NT = 256
RT = 128
F32 = jnp.float32
BF16 = jnp.bfloat16
SQRT_2_PI = math.sqrt(2.0 / math.pi)


def sequence_table():
    ids = np.arange(BLOCK)
    out = []
    for variant in range(3):
        n = BLOCK // 2**variant
        place, owner = ids % n, ids // n
        same = owner[:, None] == owner[None, :]
        angle = (place[:, None] * place[None, :] % n) * (2.0 * math.pi / n)
        factor = 1.0 / math.sqrt(n)
        cos = np.where(same, np.cos(angle) * factor, 0.0)
        sin = np.where(same, np.sin(angle) * factor, 0.0)
        out.append(np.concatenate([cos, -sin], axis=1))
    return np.stack(out).astype(np.float32).astype(BF16)


def feature_table(n):
    ids = np.arange(n)
    angle = (ids[:, None] * ids[None, :] % n) * (2.0 * math.pi / n)
    factor = 1.0 / math.sqrt(n)
    return np.concatenate([np.cos(angle), np.sin(angle)], axis=1).astype(np.float32).__mul__(np.float32(factor)).astype(BF16)


def mm(a, b):
    return lax.dot_general(a, b, (((1,), (0,)), ((), ())), preferred_element_type=F32)


def mm_t(a, b):
    return lax.dot_general(a, b, (((1,), (1,)), ((), ())), preferred_element_type=F32)


def fold(v):
    return jnp.sum(v.reshape(v.shape[0] // 8, 8, v.shape[1]), axis=0)


def gelu_both(v):
    sq = v * v
    t = jnp.tanh(SQRT_2_PI * v * (1.0 + 0.044715 * sq))
    u = 0.5 * (1.0 + t)
    slope = u + (0.5 * SQRT_2_PI) * v * (1.0 - t * t) * (1.0 + (3 * 0.044715) * sq)
    return v * u, slope


def layer_kernel(
    kind, vecs, b_in, tok_hbm, go_hbm, feat_hbm, seq_hbm, win_hbm, wout_hbm,
    out_hbm, gt_hbm, dwin_hbm, dwout_hbm, vec_out,
    tok, go, feat, seq, win, wout, hid, slope, xhat, acc, x, xt, g, gt, by, rstd, part, sems,
):
    rows, width = tok.shape
    shards = win.shape[0]
    hidden = win.shape[2]
    blocks = rows // BLOCK
    loads = [
        pltpu.make_async_copy(src, dst, sems.at[i])
        for i, (src, dst) in enumerate(
            [(tok_hbm, tok), (feat_hbm, feat), (seq_hbm, seq), (win_hbm, win), (wout_hbm, wout), (go_hbm, go)]
        )
    ]
    for c in loads:
        c.start()
    loads[0].wait()
    loads[1].wait()
    g1, s1, bo, g2, s2 = (vecs[i : i + 1, :] for i in range(5))
    tiles = [slice(i * NT, (i + 1) * NT) for i in range(width // NT)]
    htiles = [slice(i * NT, (i + 1) * NT) for i in range(hidden // NT)]

    for b in range(blocks):
        r = slice(b * BLOCK, (b + 1) * BLOCK)
        for c in tiles:
            by[0:BLOCK, c] = mm(tok[r, :], feat[:, c]).astype(BF16)
            c2 = slice(c.start + width, c.stop + width)
            by[BLOCK:, c] = mm(tok[r, :], feat[:, c2]).astype(BF16)
        if b == 0:
            loads[2].wait()
        k = kind[b]
        for c in tiles:
            xhat[r, c] = tok[r, c].astype(F32) + mm(seq[k], by[:, c])

        def norm_one(i, _, b=b):
            q = pl.ds(pl.multiple_of(b * BLOCK + i * RT, RT), RT)
            v = xhat[q, :]
            centre = v - jnp.mean(v, axis=-1, keepdims=True)
            rs = lax.rsqrt(jnp.mean(centre * centre, axis=-1, keepdims=True) + 1e-5)
            h = centre * rs
            xhat[q, :] = h
            rstd[q, :] = rs
            x[q, :] = (h * g1 + s1).astype(BF16)
            return 0

        lax.fori_loop(0, BLOCK // RT, norm_one, 0)
        for c in tiles:
            xt[c, r] = x[r, c].T

    loads[3].wait()
    loads[4].wait()

    def forward(s, _):
        for c in htiles:
            pre = mm(x[...], win[s, :, c]) + b_in[pl.ds(s, 1), c]
            a, d = gelu_both(pre)
            hid[s, :, c] = a.astype(BF16)
            slope[s, :, c] = d.astype(BF16)
        for c in tiles:
            acc[:, c] = acc[:, c] + mm(hid[s], wout[s, :, c])
        return 0

    acc[...] = jnp.zeros_like(acc)
    lax.fori_loop(0, shards, forward, 0)
    loads[5].wait()

    def norm_two(i, sums):
        q = pl.ds(pl.multiple_of(i * RT, RT), RT)
        v = xhat[q, :] * g1 + s1 + (acc[q, :] + bo)
        centre = v - jnp.mean(v, axis=-1, keepdims=True)
        rs = lax.rsqrt(jnp.mean(centre * centre, axis=-1, keepdims=True) + 1e-5)
        h = centre * rs
        tok[q, :] = (h * g2 + s2).astype(BF16)
        cot = go[q, :].astype(F32)
        dh = cot * g2
        gr = rs * (dh - jnp.mean(dh, axis=-1, keepdims=True) - h * jnp.mean(dh * h, axis=-1, keepdims=True))
        acc[q, :] = gr
        low = gr.astype(BF16)
        g[q, :] = low
        return (sums[0] + fold(cot * h), sums[1] + fold(cot), sums[2] + fold(low.astype(F32)))

    zero = jnp.zeros((8, width), F32)
    dg2, ds2, dbo = lax.fori_loop(0, rows // RT, norm_two, (zero, zero, zero))
    put_out = pltpu.make_async_copy(tok, out_hbm, sems.at[0])
    put_out.start()
    part[0:8, :] = dg2
    part[8:16, :] = ds2
    part[16:24, :] = dbo
    for b in range(blocks):
        r = slice(b * BLOCK, (b + 1) * BLOCK)
        for c in tiles:
            gt[c, r] = g[r, c].T

    def backward(s, _):
        for c in htiles:
            dwout_v[s, :, c] = mm(gt[...], hid[s, :, c]).astype(BF16)
        for c in htiles:
            gp = (mm_t(g[...], wout[s, c, :]) * slope[s, :, c].astype(F32)).astype(BF16)
            slope[s, :, c] = gp
            vec_out[pl.ds(5 + s, 1), c] = jnp.sum(fold(gp.astype(F32)), axis=0, keepdims=True)
        for c in htiles:
            dwin_v[s, :, c] = mm(xt[...], slope[s, :, c]).astype(BF16)
        return 0

    dwout_v, dwin_v = dwout_hbm, dwin_hbm
    vec_out[...] = jnp.zeros_like(vec_out)
    lax.fori_loop(0, shards, backward, 0)

    for c in tiles:
        total = acc[:, c]
        for s in range(shards):
            total = total + mm_t(slope[s], win[s, c, :])
        acc[:, c] = total

    put_out.wait()

    def back_one(i, sums):
        q = pl.ds(pl.multiple_of(i * RT, RT), RT)
        gn = acc[q, :]
        h = xhat[q, :]
        dh = gn * g1
        gs = rstd[q, :] * (dh - jnp.mean(dh, axis=-1, keepdims=True) - h * jnp.mean(dh * h, axis=-1, keepdims=True))
        acc[q, :] = gs
        tok[q, :] = gs.astype(BF16)
        return (sums[0] + fold(gn * h), sums[1] + fold(gn))

    dg1, ds1 = lax.fori_loop(0, rows // RT, back_one, (zero, zero))
    for i, v in enumerate((dg1, ds1, dbo, dg2, ds2)):
        vec_out[i : i + 1, :] = jnp.sum(v, axis=0, keepdims=True)
    for b in range(blocks):
        r = slice(b * BLOCK, (b + 1) * BLOCK)
        k = kind[b]
        for c in tiles:
            by[0:BLOCK, c] = mm(seq[k, :, 0:BLOCK], tok[r, c]).astype(BF16)
            by[BLOCK:, c] = mm(seq[k, :, BLOCK:], tok[r, c]).astype(BF16)
        for c in tiles:
            c2 = slice(c.start + width, c.stop + width)
            acc[r, c] = acc[r, c] + mm(by[0:BLOCK, :], feat[:, c]) + mm(by[BLOCK:, :], feat[:, c2])
    put = pltpu.make_async_copy(acc, gt_hbm, sems.at[0])
    put.start()
    put.wait()


def layer(kind, vecs, b_in, tokens, grad_out, feat, seq, win, wout):
    rows, width = tokens.shape
    shards, _, hidden = win.shape
    any_spec = pl.BlockSpec(memory_space=pl.ANY)
    vmem = pl.BlockSpec(memory_space=pltpu.VMEM)
    dw = jax.ShapeDtypeStruct((shards, width, hidden), BF16)
    return pl.pallas_call(
        layer_kernel,
        out_shape=(
            jax.ShapeDtypeStruct((rows, width), BF16),
            jax.ShapeDtypeStruct((rows, width), F32),
            dw,
            dw,
            jax.ShapeDtypeStruct((16, width), F32),
        ),
        in_specs=[pl.BlockSpec(memory_space=pltpu.SMEM), vmem, vmem] + [any_spec] * 6,
        out_specs=[any_spec, any_spec, vmem, vmem, vmem],
        scratch_shapes=[
            pltpu.VMEM((rows, width), BF16),
            pltpu.VMEM((rows, width), BF16),
            pltpu.VMEM(feat.shape, BF16),
            pltpu.VMEM(seq.shape, BF16),
            pltpu.VMEM(win.shape, BF16),
            pltpu.VMEM(wout.shape, BF16),
            pltpu.VMEM((shards, rows, hidden), BF16),
            pltpu.VMEM((shards, rows, hidden), BF16),
            pltpu.VMEM((rows, width), F32),
            pltpu.VMEM((rows, width), F32),
            pltpu.VMEM((rows, width), BF16),
            pltpu.VMEM((width, rows), BF16),
            pltpu.VMEM((rows, width), BF16),
            pltpu.VMEM((width, rows), BF16),
            pltpu.VMEM((2 * BLOCK, width), BF16),
            pltpu.VMEM((rows, 1), F32),
            pltpu.VMEM((24, width), F32),
            pltpu.SemaphoreType.DMA((6,)),
        ],
        compiler_params=pltpu.CompilerParams(vmem_limit_bytes=63 * 2**20),
    )(kind, vecs, b_in, tokens, grad_out, feat, seq, win, wout)


def local(
    tokens, block_kind, ln1_gain, ln1_bias, w_in, b_in, w_out, b_out, ln2_gain, ln2_bias, grad_out
):
    n_dp, n_mp = lax.axis_size("dp"), lax.axis_size("mp")
    both = ("mp", "dp")
    width, hidden = w_in.shape
    vecs = jnp.stack([ln1_gain, ln1_bias, b_out, ln2_gain, ln2_bias]).astype(F32)
    vecs = jnp.pad(vecs, ((0, 3), (0, 0)))
    bias = lax.all_gather(b_in, "mp").astype(F32)
    d = lax.axis_index("dp")
    part = width // n_dp
    mine = jnp.stack(
        [lax.dynamic_slice_in_dim(w_in, d * part, part), lax.dynamic_slice_in_dim(w_out, d * part, part)]
    )
    full = lax.all_gather(mine, both).reshape(n_mp, n_dp, 2, part, hidden)
    full = full.transpose(2, 0, 1, 3, 4).reshape(2, n_mp, width, hidden)
    feat = jnp.asarray(feature_table(width))
    seq = jnp.asarray(sequence_table())
    out, gt, dwin, dwout, vec = layer(
        block_kind, vecs, bias, tokens, grad_out, feat, seq, full[0], full[1]
    )
    dws = jnp.stack([dwin, dwout], axis=2).reshape(n_mp * width * 2, hidden)
    dws = lax.psum_scatter(dws, both, scatter_dimension=0, tiled=True)
    dws = lax.all_gather(dws, "dp", axis=0, tiled=True).reshape(width, 2, hidden)
    small = lax.psum(vec, ("dp", "mp"))
    grad_b_in = lax.dynamic_index_in_dim(small, 5 + lax.axis_index("mp"), 0, keepdims=False)
    return (
        out,
        gt,
        small[0],
        small[1],
        dws[:, 0].astype(F32),
        grad_b_in,
        dws[:, 1].astype(F32).T,
        small[2],
        small[3],
        small[4],
    )


def solution(mesh):
    in_specs = (
        P(("dp", "mp"), None),
        P(("dp", "mp")),
        P(),
        P(),
        P(None, "mp"),
        P("mp"),
        P("mp", None),
        P(),
        P(),
        P(),
        P(("dp", "mp"), None),
    )
    out_specs = (
        P(("dp", "mp"), None),
        P(("dp", "mp"), None),
        P(),
        P(),
        P(None, "mp"),
        P("mp"),
        P("mp", None),
        P(),
        P(),
        P(),
    )
    return jax.shard_map(local, mesh=mesh, in_specs=in_specs, out_specs=out_specs, check_vma=False)
```

time: 795 us -> 420 us (0.53)
  waiting for transfers between devices: 533 us -> 201 us
  matrix products: 117 us -> 0 us
  Pallas kernels: 0 us -> 66.8 us
  local copies, waits for them, and re-layouts: 27.1 us -> 65.5 us
  other arithmetic: 38 us -> 15.6 us
    all_gather x2, waiting for transfers between devices: 235 us -> 67.2 us  [the longest x1 67.2 us: local(): full = lax.all_gather(mine, both).reshape(n_mp, n_dp, 2, part, hidden)]
    reduce_scatter x2 -> x1, waiting for transfers between devices: 285 us -> 134 us  [local(): dws = lax.psum_scatter(dws, both, scatter_dimension=0, tiled=True)]
    dot_general x14 -> x0, matrix products: 117 us -> none  [the longest x4 47.9 us: times_transposed(): lax.dot_general(left, right, (((1,), (1,)), ((), ())), preferred_element_...]
    pallas_call x0 -> x1, Pallas kernels: none -> 66.8 us  [layer(): pl.pallas_call(layer_kernel, out_shape=(jax.ShapeDtypeStruct((rows, width...]
    another operation x0 -> x8, local copies, waits for them, and re-layouts: none -> 22.9 us  [the longest x1 18.5 us: local(): dws = jnp.stack([dwin, dwout], axis=2).reshape(n_mp * width * 2, hidden)]
    reshape x2, local copies, waits for them, and re-layouts: 4.77 us -> 24.8 us  [the longest x1 20 us: local(): dws = jnp.stack([dwin, dwout], axis=2).reshape(n_mp * width * 2, hidden)]
    reduce_sum x9 -> x0, other arithmetic: 17.7 us -> none  [the longest x4 9.63 us: layer_norm(): centre = values - jnp.mean(values, axis=-1, keepdims=True)]
    psum x2 -> x1, blocking collectives: 57.5 us -> 40.6 us  [local(): small = lax.psum(vec, ('dp', 'mp'))]
  transfers between devices with their start and end apart: 5 -> 3, of which waited for: 5 -> 2; matrix products, arithmetic and copies ran while one was open for 7% -> 1% of each run, Pallas kernels for 0% -> 0%
where the time goes in v1:
time: 420 us; the launch traced here: 419 us
  waiting for transfers between devices  201 us (48%)
  Pallas kernels  66.8 us (16%)
  local copies, waits for them, and re-layouts  65.5 us (16%)
  blocking collectives  55.4 us (13%)
  other arithmetic  15.6 us (4%)
  between operations  13.8 us (3%)
    reduce_scatter x1, waiting for transfers between devices, local(): dws = lax.psum_scatter(dws, both, scatter_dimension=0, tiled=True)  134 us
    all_gather x1, waiting for transfers between devices, local(): full = lax.all_gather(mine, both).reshape(n_mp, n_dp, 2, part, hidden)  67.2 us
    pallas_call x1, Pallas kernels, layer(): pl.pallas_call(layer_kernel, out_shape=(jax.ShapeDtypeStruct((rows, width...  66.8 us
    psum x1, blocking collectives, local(): small = lax.psum(vec, ('dp', 'mp'))  40.6 us
    reshape x1, local copies, waits for them, and re-layouts, local(): dws = jnp.stack([dwin, dwout], axis=2).reshape(n_mp * width * 2, hidden)  20 us
    another operation x1, local copies, waits for them, and re-layouts, local(): dws = jnp.stack([dwin, dwout], axis=2).reshape(n_mp * width * 2, hidden)  18.5 us
    all_gather x1, blocking collectives, local(): bias = lax.all_gather(b_in, 'mp').astype(F32)  14.7 us
  transfers between devices with their start and end apart: 3, of which 2 were waited for; matrix products, arithmetic and copies ran while one was open for 1% of the time, Pallas kernels for 0%

profile of v1, /device:TPU:0, one launch (start us, length us, event | category | flops | bytes accessed | tf_op | source)
XLA Modules:
  0.0 418.6 jit_solution(16690611877089276376)
XLA Ops:
  7.2 1.0 dynamic-slice_bitcast_fusion
  8.2 0.7 pad_maximum_fusion.1
  9.1 0.7 stack.36
  9.7 0.7 stack.37
  10.4 0.7 reshape.47
  11.1 0.7 stack.38
  11.8 0.7 stack.39
  12.5 0.7 stack.40
  13.2 14.7 %all-gather.2 = bf16[4,1,768]{2,1,0:T(2,128)(2,1)S(1)} all-gather(bf16[1,1,768]{2,1,0:T(2,128)(2,1)S(1)} %reshape.47), channel_id=2, replica_groups=mesh['dp'=8,'mp'=4] {'mp'}, dimensions={0}, use_global_device_ids=true | all-gather | bytes 7680 | tf_op jit(solution)/shard_map/all_gather | solution.py:255
  27.9 0.6 pad_convert_fusion.vecs
  28.5 0.6 bitcast_convert_fusion.b_in
  29.1 67.2 %all-gather.8.cloned.1.call-done = bf16[64,96,768]{2,1,0:T(8,128)(2,1)} async-done(((bf16[2,96,768]{2,1,0:T(8,128)(2,1)}), bf16[64,96,768]{2,1,0:T(8,128)(2,1)}) %all-gather.8.cloned.1.call-update) | async-done | bytes 9437200 | tf_op jit(solution)/shard_map/all_gather | solution.py:261
  96.3 8.0 %fusion = (bf16[1,4,8,96,768]{4,3,0,2,1:T(8,128)(2,1)}, bf16[1,4,8,96,768]{4,3,0,2,1:T(8,128)(2,1)}) fusion(bf16[2,4,8,96,768]{4,3,0,2,1:T(8,128)(2,1)} %bitcast.23), kind=kLoop, calls=%fused_computation.15 | loop fusion | bytes 18874368 | tf_op jit(solution)/shard_map/slice | solution.py:266
  104.3 66.8 %shard_map.204 = (bf16[1024,768]{1,0:T(8,128)(2,1)}, f32[1024,768]{1,0:T(8,128)}, bf16[4,768,768]{2,1,0:T(8,128)(2,1)}, bf16[4,768,768]{2,1,0:T(8,128)(2,1)}, f32[16,768]{1,0:T(8,128)}) custom-call(s32[2]{0:T(128)} %kind.1, f32[8,768]{1,0:T(8,128)} %pad_convert_fusion.vecs, f32[4,768]{1,0:T(4,128)} %bitcast_convert_fusion.b_in, bf16[1024,768]{1,0:T(8,128)(2,1)} %tok_hbm.1, ...), custom_call_target="tpu_custom_call" | custom-call | tf_op jit(solution)/shard_map/pallas_call | solution.py:212
  171.1 8.3 %pad_maximum_fusion = bf16[4,768,2,768]{3,1,0,2:T(8,128)(2,1)} fusion(bf16[4,768,1,768]{3,1,0,2:T(8,128)(2,1)} %bitcast.25, bf16[4,768,1,768]{3,1,0,2:T(8,128)(2,1)} %bitcast.24), kind=kLoop, calls=%fused_computation | loop fusion | flops 4718592 | bytes 18874368 | tf_op jit(solution)/shard_map/stack | solution.py:268
  179.4 18.5 %copy.26 = bf16[4,768,2,768]{3,2,1,0:T(2,128)(2,1)} copy(bf16[4,768,2,768]{3,1,0,2:T(8,128)(2,1)} %pad_maximum_fusion) | data formatting | bytes 18874368 | tf_op jit(solution)/shard_map/stack | solution.py:268
  197.9 20.0 %reshape.39 = bf16[6144,768]{1,0:T(8,128)(2,1)} reshape(bf16[4,768,2,768]{3,2,1,0:T(2,128)(2,1)} %copy.26) | data formatting | bytes 18874368 | tf_op jit(solution)/shard_map/reshape | solution.py:268
  217.9 134.2 %reduce-scatter.2.cloned.1.call-done = bf16[192,768]{1,0:T(8,128)(2,1)} async-done(((bf16[6144,768]{1,0:T(8,128)(2,1)}), bf16[192,768]{1,0:T(8,128)(2,1)}) %reduce-scatter.2.cloned.1.call-update) | async-done | bytes 294928 | tf_op jit(solution)/shard_map/reduce_scatter | solution.py:269
  352.2 40.6 %psum.7 = f32[16,768]{1,0:T(8,128)S(1)} all-reduce(f32[16,768]{1,0:T(8,128)S(1)} %copy-done.1), channel_id=1, replica_groups=mesh['dp'=8,'mp'=4] {'dp','mp'}, use_global_device_ids=true, to_apply=%region_0.1 | all-reduce | flops 12288 | bytes 98304 | tf_op jit(solution)/shard_map/psum | solution.py:271
  392.8 0.6 slice_reduce_fusion
  393.5 4.8 %reshape.40 = bf16[768,2,768]{2,1,0:T(2,128)(2,1)S(1)} reshape(bf16[1536,768]{1,0:T(8,128)(2,1)} %all-gather.6.cloned.1.call-done) | data formatting | bytes 4718592 | tf_op jit(solution)/shard_map/reshape | solution.py:270
  398.3 5.4 %slice_convert_fusion = (f32[768,1,768]{2,1,0:T(1,128)}, f32[768,1,768]{2,1,0:T(1,128)}) fusion(bf16[768,2,768]{2,1,0:T(2,128)(2,1)S(1)} %reshape.40), kind=kLoop, calls=%fused_computation.1 | loop fusion | flops 1179648 | bytes 7077888 | tf_op jit(solution)/shard_map/transpose | solution.py:280
  403.7 6.8 %copy.30 = f32[768,1,768]{0,2,1:T(8,128)} copy(f32[768,1,768]{2,1,0:T(1,128)} %get-tuple-element.48) | data formatting | bytes 4718592 | tf_op jit(solution)/shard_map/transpose | solution.py:280
  410.5 1.6 copy.33
  (12 shorter events, 0.2 us)
Async XLA Ops:
  7.2 89.1 %all-gather.8.cloned.1.call-start = ((), (), s32[]{:S(2)}) async-start(), calls=%async_computation.3 | async-start | bytes 9732096 | tf_op jit(solution)/shard_map/all_gather | solution.py:261
  9.0 343.1 %reduce-scatter.2.cloned.1.call-start = ((), (), s32[]{:S(2)}) async-start(), calls=%async_computation.1 | async-start | bytes 9732096 | tf_op jit(solution)/shard_map/reduce_scatter | solution.py:269
  217.8 134.3 %copy-start.1 = (f32[16,768]{1,0:T(8,128)S(1)}, f32[16,768]{1,0:T(8,128)}, u32[]{:S(2)}) copy-start(f32[16,768]{1,0:T(8,128)} %get-tuple-element.17) | copy-start | bytes 147460
  217.9 175.6 %all-gather.6.cloned.1.call-start = ((), (), s32[]{:S(2)}) async-start(), calls=%async_computation.2 | async-start | bytes 2654208 | tf_op jit(solution)/shard_map/all_gather | solution.py:270
  403.7 6.8 %copy-start = (f32[768,1,768]{2,1,0:T(1,128)S(1)}, f32[768,1,768]{2,1,0:T(1,128)}, u32[]{:S(2)}) copy-start(f32[768,1,768]{2,1,0:T(1,128)} %get-tuple-element.49) | copy-start | bytes 7077892
Sparse Core Ops, SparseCore 0:
  11.5 84.7 all-gather.7
  218.0 134.0 reduce-scatter.1
  354.2 28.3 all-gather.5
